TPU v7x, 256 devices: a whole 4x4x8 slice. The times are simulated.
256 devices in a mesh: proto: 64 (over y, z, core), batch: 4 (over x).
Axes of the slice: x: 4, y: 4, z: 8, core: 2. Of those that a mesh axis runs over, the one named last changes fastest.
Arguments:
- features: bfloat16 [2, 4096, 1024], P(None, 'batch', 'proto'), may hold values from -240 to 240
- prototypes: bfloat16 [1024, 65536], P(None, 'proto'), may hold values from -1.5 to 1.5
Outputs:
- proto_grad: float32 [1024, 65536], P('batch', 'proto')
- loss_value: float32 [], replicated
All inputs are finite; a program needn't handle non-finite values.
Results may differ from a plain program's by a relative error of at most 0.003.
Values may be sent and summed in bfloat16 or wider, within the bound.
A program may use at most 64 MiB of HBM per device.

v0:
```python
import jax
import jax.numpy as jnp
from jax import lax
from jax.sharding import PartitionSpec as P

ITERS = 3


eps_assign = 0.05
heat_parameter = 0.1


def per_device(features, prototypes):
    highest = lax.Precision.HIGHEST
    view_count = features.shape[0]
    row_count = features.shape[1]
    width_dev = prototypes.shape[1]
    feature_width = prototypes.shape[0]
    proto_wide = prototypes.astype(jnp.float32)
    proto_scale = lax.rsqrt(jnp.sum(proto_wide * proto_wide, axis=0) + 1e-06)
    unit_wide = proto_wide * proto_scale[None, :]
    unit_protos = unit_wide.astype(jnp.bfloat16)
    gathered = lax.all_gather(features, "proto", axis=2, tiled=True)
    squares = jnp.sum(jnp.square(gathered.astype(jnp.float32)), axis=2)
    raw_scores = jnp.einsum(
        "vbd,dk->vbk", gathered, unit_protos, preferred_element_type=jnp.float32
    )
    sample_rescaling = lax.rsqrt(squares + 1e-06)
    centroid_affinity_matrix = raw_scores * sample_rescaling[:, :, None]
    peaked_affinity_matrix = jnp.exp(centroid_affinity_matrix / heat_parameter)
    centroid_mass_vector = lax.psum(jnp.sum(peaked_affinity_matrix, axis=2), "proto")
    kernel = jnp.exp(centroid_affinity_matrix / eps_assign)
    sample_factor = jnp.ones((view_count, row_count), jnp.float32)
    proto_factor = jnp.ones((view_count, width_dev), jnp.float32)
    for iteration in range(ITERS):
        proto_mass = jnp.einsum("vbk,vb->vk", kernel, sample_factor, precision=highest)
        proto_factor = 1.0 / lax.psum(proto_mass, "batch")
        sample_sum = jnp.einsum("vbk,vk->vb", kernel, proto_factor, precision=highest)
        sample_factor = 1.0 / lax.psum(sample_sum, "proto")
    assign = kernel * proto_factor[:, None, :] * sample_factor[:, :, None]
    traded_prediction_cost = assign[::-1]
    logarithmic_probabilities = (
        centroid_affinity_matrix / heat_parameter - jnp.log(centroid_mass_vector)[:, :, None]
    )
    estimated_membership = peaked_affinity_matrix / centroid_mass_vector[:, :, None]
    local_loss = jnp.sum(traded_prediction_cost * logarithmic_probabilities)
    total_rows = row_count * lax.axis_size("batch")
    loss_value = -lax.psum(local_loss, ("proto", "batch")) / (2.0 * total_rows)
    affinity_slope_matrix = (
        (estimated_membership - traded_prediction_cost)
        / heat_parameter
        * sample_rescaling[:, :, None]
    ).astype(jnp.bfloat16)
    proto_delta = jnp.einsum(
        "vbd,vbk->dk", gathered, affinity_slope_matrix, preferred_element_type=jnp.float32
    )
    share_rows = feature_width // lax.axis_size("batch")
    share_start = lax.axis_index("batch") * share_rows
    summed = lax.psum(proto_delta, "batch")
    inner_sums = jnp.sum(unit_wide * summed, axis=0)
    whole_grad = proto_scale[None, :] * (summed - unit_wide * inner_sums[None, :])
    proto_grad = lax.dynamic_slice_in_dim(whole_grad, share_start, share_rows, 0)
    return (proto_grad, loss_value)


def solution(mesh):
    placed = (P(None, "batch", "proto"), P(None, "proto"))
    return jax.shard_map(
        per_device,
        mesh=mesh,
        in_specs=placed,
        out_specs=(P("batch", "proto"), P()),
        check_vma=False,
    )
```

profile of v0, /device:TPU:1, one launch (start us, length us, event | category | flops | bytes accessed | tf_op | source)
XLA Modules:
  0.0 807.3 jit_solution(16461789056464225297)
XLA Ops:
  7.2 0.0 all-gather.2.cloned.1.call-start
  7.2 0.7 all-gather.2.cloned.1.call-update
  7.9 0.0 all-reduce.3.cloned.1.call-start
  7.9 2.9 copy.4
  10.8 0.5 fusion.17
  11.3 82.9 %all-gather.2.cloned.1.call-done = bf16[2,1024,1024]{1,2,0:T(8,128)(2,1)} async-done(((bf16[2,1024,16]{1,2,0:T(8,128)(2,1)}), bf16[2,1024,1024]{1,2,0:T(8,128)(2,1)}) %all-gather.2.cloned.1.call-update) | async-done | bytes 4194320 | tf_op jit(solution)/shard_map/all_gather | solution.py:23
  94.2 3.3 multiply_reduce_fusion
  97.5 6.6 bitcast_reduce_fusion
  104.1 0.0 copy-start
  104.1 3.2 copy-done
  107.3 8.1 %fusion.11 = f32[2,1,1024]{2,1,0:T(1,128)S(1)} fusion(f32[1024,2,1024]{2,0,1:T(8,128)S(1)} %get-tuple-element.13, f32[2,1024]{1,0:T(2,128)S(1)} %get-tuple-element.11), kind=kOutput, calls=%fused_computation.13 | convolution fusion | flops 29360128 | bytes 8404992 | tf_op jit(solution)/shard_map/vbk,vb->vk/dot_general | solution.py:36
  115.4 8.7 %psum.64 = f32[2,1024]{1,0:T(2,128)S(1)} all-reduce(f32[2,1024]{1,0:T(2,128)S(1)} %bitcast.70), channel_id=1, replica_groups=mesh['proto'=64,'batch'=4] {'batch'}, use_global_device_ids=true, to_apply=%region_4.0 | all-reduce | flops 2048 | bytes 16384 | tf_op jit(solution)/shard_map/psum | solution.py:37
  124.1 7.8 fusion.9
  131.9 127.7 %psum.65 = f32[2,1024]{1,0:T(2,128)S(1)} all-reduce(f32[2,1024]{1,0:T(2,128)S(1)} %bitcast.71), channel_id=1, replica_groups=mesh['proto'=64,'batch'=4] {'proto'}, use_global_device_ids=true, to_apply=%region_5.0 | all-reduce | flops 2048 | bytes 16384 | tf_op jit(solution)/shard_map/psum | solution.py:39
  259.6 10.5 %fusion.7 = f32[2,1,1024]{2,1,0:T(1,128)S(1)} fusion(f32[2,1024,1]{1,0,2:T(2,128)S(1)} %divide_bitcast_fusion.2, f32[1024,2,1024]{2,0,1:T(8,128)} %copy-done, f32[2,1024]{1,0:T(2,128)S(1)} %get-tuple-element.11), kind=kOutput, calls=%fused_computation.9 | convolution fusion | flops 29360128 | bytes 8413184 | tf_op jit(solution)/shard_map/vbk,vb->vk/dot_general | solution.py:36
  270.1 6.1 psum.66
  276.2 7.8 fusion.5
  284.0 128.3 %psum.67 = f32[2,1024]{1,0:T(2,128)S(1)} all-reduce(f32[2,1024]{1,0:T(2,128)S(1)} %bitcast.73), channel_id=1, replica_groups=mesh['proto'=64,'batch'=4] {'proto'}, use_global_device_ids=true, to_apply=%region_7.0 | all-reduce | flops 2048 | bytes 16384 | tf_op jit(solution)/shard_map/psum | solution.py:39
  412.4 10.5 %fusion.3 = f32[2,1,1024]{2,1,0:T(1,128)S(1)} fusion(f32[2,1024,1]{1,0,2:T(2,128)S(1)} %divide_bitcast_fusion, f32[1024,2,1024]{2,0,1:T(8,128)} %copy-done, f32[2,1024]{1,0:T(2,128)S(1)} %get-tuple-element.11), kind=kOutput, calls=%fused_computation.5 | convolution fusion | flops 29360128 | bytes 8413184 | tf_op jit(solution)/shard_map/vbk,vb->vk/dot_general | solution.py:36
  422.9 7.8 psum.68
  430.7 7.8 fusion.1
  438.5 243.2 %all-reduce = (f32[2,1024]{1,0:T(2,128)S(1)}, f32[2,1024]{1,0:T(2,128)S(1)}) all-reduce(f32[2,1024]{1,0:T(2,128)S(1)} %bitcast.69, f32[2,1024]{1,0:T(2,128)S(1)} %get-tuple-element.12), channel_id=1, replica_groups=mesh['proto'=64,'batch'=4] {'proto'}, use_global_device_ids=true, to_apply=%region_9.0 | all-reduce | flops 4096 | bytes 32768 | tf_op jit(solution)/shard_map/psum | solution.py:39
  681.8 4.3 fusion.13
  686.1 0.0 copy-start.1
  686.1 5.9 fusion
  692.0 0.0 copy-done.1
  692.0 6.1 convolution_bitcast_fusion
  698.1 0.0 all-reduce.3.cloned.1.call-update
  698.1 77.7 %psum.71 = f32[]{:T(128)} all-reduce(f32[]{:T(128)} %get-tuple-element.6), channel_id=1, replica_groups=mesh['proto'=64,'batch'=4] {'proto','batch'}, use_global_device_ids=true, to_apply=%region_13.0 | all-reduce | flops 1 | bytes 8 | tf_op jit(solution)/shard_map/psum | solution.py:48
  776.5 17.0 %all-reduce.3.cloned.1.call-done = f32[1024,1024]{0,1:T(8,128)} async-done(((f32[1024,1024]{0,1:T(8,128)}), f32[1024,1024]{0,1:T(8,128)}) %all-reduce.3.cloned.1.call-update) | async-done | bytes 4194320 | tf_op jit(solution)/shard_map/psum | solution.py:59
  793.5 2.9 multiply_reduce_fusion.1
  796.4 1.6 fusion.21
  798.0 1.3 copy.5
  (16 shorter events, 0.2 us)
Async XLA Ops:
  7.2 87.0 %all-gather.2.cloned.1.call-start = ((), (), s32[]{:S(2)}) async-start(), calls=%async_computation | async-start | bytes 4259840 | tf_op jit(solution)/shard_map/all_gather | solution.py:23
  7.9 785.6 %all-reduce.3.cloned.1.call-start = ((), (), s32[]{:S(2)}) async-start(), calls=%async_computation.1 | async-start | bytes 8388608 | tf_op jit(solution)/shard_map/psum | solution.py:59
  104.1 3.2 copy-start
  686.1 5.9 copy-start.1
Sparse Core Ops, SparseCore 0:
  10.8 83.3 all-gather.1
  698.2 95.1 all-reduce.2
where the time goes:
time: 808 us; the launch traced here: 807 us
  blocking collectives  600 us (74%)
  waiting for transfers between devices  101 us (12%)
  matrix products  65 us (8%)
  other arithmetic  18.6 us (2%)
  between operations  16 us (2%)
    psum x3, blocking collectives, per_device(): sample_factor = 1.0 / lax.psum(sample_sum, 'proto')  499 us
    all_gather x1, waiting for transfers between devices, per_device(): gathered = lax.all_gather(features, 'proto', axis=2, tiled=True)  82.9 us
    psum x1, blocking collectives, per_device(): loss_value = -lax.psum(local_loss, ('proto', 'batch')) / (2.0 * total_rows)  77.7 us
    dot_general x3, matrix products, per_device(): jnp.einsum('vbk,vb->vk', kernel, sample_factor, precision=highest)  29 us
    dot_general x3, matrix products, per_device(): jnp.einsum('vbk,vk->vb', kernel, proto_factor, precision=highest)  23.3 us
    psum x3, blocking collectives, per_device(): proto_factor = 1.0 / lax.psum(proto_mass, 'batch')  22.6 us
    psum x1, waiting for transfers between devices, per_device(): summed = lax.psum(proto_delta, 'batch')  17 us
  transfers between devices with their start and end apart: 2, of which 2 were waited for; matrix products, arithmetic and copies ran while one was open for 0% of the time, Pallas kernels for 0%

commit v1 on v0

v1 whole, which is shorter than its diff:
```python
import functools
import math

import jax
import jax.numpy as jnp
from jax import lax
from jax.experimental import pallas as pl
from jax.experimental.pallas import tpu as pltpu
from jax.sharding import PartitionSpec as P

ITERS = 3
NX, NY, NZ, NC = 4, 4, 8, 2
VIEWS = 2
D = 1024
KD = 1024
RD = 1024
ROWS = NX * RD
PIECE = 16
CHUNK = 256
CHUNKS = KD // CHUNK
HEAT = 10.0
EXP2_SCALE = 10.0 * math.log2(math.e)
F32 = jnp.float32
BF16 = jnp.bfloat16
NT = (((1,), (1,)), ((), ()))


def kernel(feat_ref, proto_ref, grad_ref, loss_ref, ft, pv, ut, sc, kn, sg, scale, rscale, tot, part, xbuf, ybuf, zbuf,
           lx, ly, lz, inner, snd2, sndp, sndm, r1p, r1m, recp, recm, dp, dm, down,
           in_sem, z_s, z_r, y_s, y_r, f_s, f_r, c_s, c_r, xs_s, xs_r, ys_s, ys_r, zs_s, zs_r,
           lx_s, lx_r, ly_s, ly_r, lz_s, lz_r, in_s, in_r, h_s, h_r, d_s, d_r, e_s, e_r):
    xi = lax.axis_index("batch")
    me = lax.axis_index("proto")
    c = lax.rem(me, NC)
    z = lax.rem(lax.div(me, NC), NZ)
    y = lax.div(me, NC * NZ)

    def at_y(dy):
        return lax.rem(y + dy % NY, NY)

    def at_z(dz):
        return lax.rem(z + dz % NZ, NZ)

    def at_x(dx):
        return lax.rem(xi + dx % NX, NX)

    def dev(dx=0, dy=0, dz=0, dc=0):
        return ((at_y(dy) * NZ + at_z(dz)) * NC + lax.rem(c + dc, NC), at_x(dx))

    yc_peers = [(dy, dc) for dy in range(NY) for dc in range(NC) if dy or dc]
    z_order = [1, 7, 2, 6, 3, 5, 4]

    load_p = pltpu.make_async_copy(proto_ref, pv, in_sem.at[0])
    load_p.start()
    load_f = pltpu.make_async_copy(feat_ref, ft.at[:, y, z, c], in_sem.at[1])
    load_f.start()

    barrier = pltpu.get_barrier_semaphore()
    peers = [dev(dy=dy, dc=dc) for dy, dc in yc_peers]
    peers += [dev(dz=dz) for dz in z_order] + [dev(dx=dx) for dx in (1, 2, 3)]
    for peer in peers:
        pl.semaphore_signal(barrier, inc=1, device_id=peer, device_id_type=pl.DeviceIdType.MESH)

    load_p.wait()

    def square_step(i, acc):
        v = pv[pl.ds(pl.multiple_of(i * 16, 16), 16), :].astype(F32)
        return acc + v * v

    sq = lax.fori_loop(0, D // 16, square_step, jnp.zeros((16, KD), F32))
    scale[...] = lax.rsqrt(jnp.sum(sq, axis=0, keepdims=True) + 1e-6)

    def unit_step(i, _):
        rows = pl.ds(pl.multiple_of(i * 128, 128), 128)
        for kb in range(KD // 128):
            cols = slice(kb * 128, kb * 128 + 128)
            ut[cols, rows] = (pv[rows, cols].astype(F32) * scale[:, cols]).T.astype(BF16)
        return 0

    lax.fori_loop(0, D // 128, unit_step, 0)
    load_f.wait()
    pl.semaphore_wait(barrier, len(peers))

    sends = []

    def copy(src, dst, ssem, rsem, to):
        return pltpu.make_async_remote_copy(
            src_ref=src, dst_ref=dst, send_sem=ssem, recv_sem=rsem, device_id=to, device_id_type=pl.DeviceIdType.MESH
        )

    def send(src, dst, ssem, rsem, to):
        cp = copy(src, dst, ssem, rsem, to)
        cp.start()
        sends.append(cp)

    def arrived(dst, ssem, rsem):
        copy(dst, dst, ssem, rsem, dev(dc=1)).wait_recv()

    def piece(dy, dz, core=None):
        return ft.at[:, at_y(dy), at_z(dz), c if core is None else core]

    def to_sibling(dy, dz):
        send(piece(dy, dz), piece(dy, dz), c_s.at[dy, dz], c_r.at[dy, dz], dev(dc=1))

    def along_y(dz):
        for side, dy in ((0, 1), (1, 3)):
            send(piece(0, dz), piece(0, dz), y_s.at[side, dz], y_r.at[(-dy) % NY, dz], dev(dy=dy))

    def half(dy, dz, view):
        return ft.at[view, at_y(dy), at_z(dz), c]

    along_y(0)
    for dz in z_order:
        send(piece(0, 0), piece(0, 0), z_s.at[dz], z_r.at[(-dz) % NZ], dev(dz=dz))
    to_sibling(0, 0)

    def pass_on_y(dz):
        for side, dy in ((0, 3), (1, 1)):
            arrived(piece(dy, dz), y_s.at[0, 0], y_r.at[dy, dz])
            send(half(dy, dz, side), half(dy, dz, side), f_s.at[side, dz], f_r.at[side, dz], dev(dy=-dy))
            to_sibling(dy, dz)

    pass_on_y(0)
    for i, dz in enumerate(z_order):
        arrived(piece(0, dz), z_s.at[0], z_r.at[dz])
        along_y(dz)
        to_sibling(0, dz)
    for dz in z_order:
        pass_on_y(dz)
    for dz in [0] + z_order:
        for side in range(2):
            arrived(half(2, dz, side), f_s.at[0, 0], f_r.at[side, dz])
        to_sibling(2, dz)
    for dy in (0, 1, 3, 2):
        for dz in [0] + z_order:
            arrived(piece(dy, dz, 1 - c), c_s.at[0, 0], c_r.at[dy, dz])

    def row_square(i, acc):
        new = []
        for v in range(VIEWS):
            val = ft[v, lax.div(i, 16), lax.rem(lax.div(i, 2), 8), lax.rem(i, 2)].astype(F32)
            new.append(acc[v] + val * val)
        return tuple(new)

    acc = lax.fori_loop(0, D // PIECE, row_square, (jnp.zeros((16, RD), F32),) * 2)
    for v in range(VIEWS):
        rscale[v] = lax.rsqrt(jnp.sum(acc[v], axis=0, keepdims=True) + 1e-6)

    def lane_sum_row(tiles):
        return jnp.sum(tiles.T, axis=0, keepdims=True)

    tot[...] = jnp.zeros_like(tot)
    for v in range(VIEWS):
        def score_step(i, _, v=v):
            rows = pl.ds(pl.multiple_of(i * 128, 128), 128)
            raw = jnp.dot(ut[rows, :], ft[v].reshape(D, RD), preferred_element_type=F32)
            s = raw * rscale[v]
            sc[v, rows, :] = s
            e = jnp.exp2(s * EXP2_SCALE)
            k = e * e
            kn[v, rows, :] = k
            mass = k[:, 0:128]
            for j in range(1, RD // 128):
                mass = mass + k[:, j * 128:(j + 1) * 128]
            xbuf[0, 0, v, pl.ds(i, 1), :] = lane_sum_row(mass)
            for j in range(RD // 128):
                tot[v, j:j + 1, :] += jnp.sum(e[:, j * 128:(j + 1) * 128], axis=0, keepdims=True)
            return 0

        lax.fori_loop(0, KD // 128, score_step, 0)

    def column(buf, v, kb):
        return jnp.broadcast_to(buf[v, pl.ds(kb, 1), :], (128, 128)).T

    def sum_slots(buf, order):
        total = buf[order[0]]
        for i in order[1:]:
            total = total + buf[i]
        return total

    for t in range(ITERS):
        if t:
            for v in range(VIEWS):
                def mass_step(i, _, v=v):
                    rows = pl.ds(pl.multiple_of(i * 128, 128), 128)
                    mass = kn[v, rows, 0:128] * part[0, v, 0:1, :]
                    for j in range(1, RD // 128):
                        mass = mass + kn[v, rows, j * 128:(j + 1) * 128] * part[0, v, j:j + 1, :]
                    xbuf[t, 0, v, pl.ds(i, 1), :] = lane_sum_row(mass)
                    return 0

                lax.fori_loop(0, KD // 128, mass_step, 0)
        for dx in (1, 2, 3):
            send(xbuf.at[t, 0], xbuf.at[t, NX - dx], xs_s.at[t, dx], xs_r.at[t, NX - dx], dev(dx=dx))
        for dx in (1, 2, 3):
            arrived(xbuf.at[t, dx], xs_s.at[t, dx], xs_r.at[t, dx])
        part[1] = 1.0 / sum_slots(xbuf.at[t], range(NX))
        for v in range(VIEWS):
            def sample_step(i, acc, v=v):
                rows = pl.ds(pl.multiple_of(i * 128, 128), 128)
                col = column(part.at[1], v, i)
                return tuple(
                    acc[j] + jnp.sum((kn[v, rows, j * 128:(j + 1) * 128] * col).reshape(16, 8, 128), axis=0)
                    for j in range(RD // 128)
                )

            acc = lax.fori_loop(0, KD // 128, sample_step, (jnp.zeros((8, 128), F32),) * 8)
            for j in range(RD // 128):
                ybuf[t, 0, v, j:j + 1, :] = jnp.sum(acc[j], axis=0, keepdims=True)
        if t == 0:
            ybuf[t, 0, 2:4] = tot[...]
        n = 4 if t == 0 else 2
        for i, (dy, dc) in enumerate(yc_peers):
            j = yc_peers.index(((-dy) % NY, dc))
            send(ybuf.at[t, 0, 0:n], ybuf.at[t, 1 + j, 0:n], ys_s.at[t, i], ys_r.at[t, j], dev(dy=dy, dc=dc))
        for i in range(len(yc_peers)):
            arrived(ybuf.at[t, 1 + i, 0:n], ys_s.at[t, i], ys_r.at[t, i])
        zbuf[t, 0, 0:n] = sum_slots(ybuf.at[t, :, 0:n], range(8))
        for dz in z_order:
            send(zbuf.at[t, 0, 0:n], zbuf.at[t, NZ - dz, 0:n], zs_s.at[t, dz], zs_r.at[t, NZ - dz], dev(dz=dz))
        for dz in z_order:
            arrived(zbuf.at[t, dz, 0:n], zs_s.at[t, dz], zs_r.at[t, dz])
        sums = sum_slots(zbuf.at[t, :, 0:n], range(NZ))
        part[0] = 1.0 / sums[0:2]
        if t == 0:
            tot[...] = sums[2:4]

    factor, proto_factor = part.at[0], part.at[1]
    loss_acc = jnp.zeros((8, 128), F32)
    for v in range(VIEWS):
        loss_acc += jnp.log(tot[v]) * factor[1 - v] * ybuf[ITERS - 1, 0, 1 - v]
    loss_acc = -loss_acc

    def grad_block(dx, cols):
        out = None
        for v in range(VIEWS):
            lhs = ft[v, at_x(dx)].reshape(CHUNK, RD)
            d = lax.dot_general(lhs, sg[v, cols, :], NT, preferred_element_type=F32)
            out = d if out is None else out + d
        return out

    def weigh(dx, cols, delta):
        rows = pl.ds(pl.multiple_of(at_x(dx) * CHUNK, CHUNK), CHUNK)
        return jnp.sum(pv[rows, cols].astype(F32) * delta, axis=0, keepdims=True)

    for kc in range(CHUNKS):
        cols = slice(kc * CHUNK, (kc + 1) * CHUNK)

        def slope_step(i, acc, kc=kc):
            kb = kc * 2 + i
            rows = pl.ds(pl.multiple_of(kb * 128, 128), 128)
            for v in range(VIEWS):
                col = column(proto_factor, 1 - v, kb)
                for j in range(RD // 128):
                    lanes = slice(j * 128, (j + 1) * 128)
                    heated = rscale[v, :, lanes] * HEAT
                    s = sc[v, rows, lanes]
                    assign = kn[1 - v, rows, lanes] * col * factor[1 - v, j:j + 1, :]
                    pred = jnp.exp2(s * EXP2_SCALE) * (heated / tot[v, j:j + 1, :])
                    sg[v, rows, lanes] = (pred - assign * heated).astype(BF16)
                    acc = acc + jnp.sum((assign * s).reshape(16, 8, 128), axis=0) * HEAT
            return acc

        loss_acc = lax.fori_loop(0, 2, slope_step, loss_acc)
        delta = grad_block(2, cols)
        snd2[:, cols] = delta.astype(BF16)
        inner[0, :, cols] = weigh(2, cols, delta)
        send(snd2.at[0:128, cols], r1p.at[:, cols], h_s.at[0, kc], h_r.at[0, kc], dev(dx=1))
        send(snd2.at[128:256, cols], r1m.at[:, cols], h_s.at[1, kc], h_r.at[1, kc], dev(dx=3))

    ly[me_slot(y, c)] = loss_acc
    for i, (dy, dc) in enumerate(yc_peers):
        j = yc_peers.index(((-dy) % NY, dc))
        send(ly.at[me_slot(y, c)], ly.at[me_slot(y, c)], ly_s.at[i], ly_r.at[j], dev(dy=dy, dc=dc))

    for kc in range(CHUNKS):
        cols = slice(kc * CHUNK, (kc + 1) * CHUNK)
        dplus = grad_block(1, cols)
        dp[:, cols] = dplus
        sndp[128:256, cols] = dplus[128:256].astype(BF16)
        send(sndp.at[128:256, cols], recp.at[128:256, cols], d_s.at[0, kc], d_r.at[0, kc], dev(dx=1))
        dminus = grad_block(3, cols)
        dm[:, cols] = dminus
        sndm[0:128, cols] = dminus[0:128].astype(BF16)
        send(sndm.at[0:128, cols], recm.at[0:128, cols], d_s.at[1, kc], d_r.at[1, kc], dev(dx=3))
        own = grad_block(0, cols)
        down[:, cols] = own
        inner[0, :, cols] += weigh(1, cols, dplus) + weigh(3, cols, dminus) + weigh(0, cols, own)
    for dx in (1, 2, 3):
        send(inner.at[0], inner.at[NX - dx], in_s.at[dx], in_r.at[NX - dx], dev(dx=dx))

    for i, (dy, dc) in enumerate(yc_peers):
        slot = me_slot(at_y(dy), lax.rem(c + dc, NC))
        arrived(ly.at[slot], ly_s.at[i], ly_r.at[i])
    lz[z] = sum_slots(ly, range(8))
    for dz in z_order:
        send(lz.at[z], lz.at[z], lz_s.at[dz], lz_r.at[NZ - dz], dev(dz=dz))

    for kc in range(CHUNKS):
        cols = slice(kc * CHUNK, (kc + 1) * CHUNK)
        arrived(r1p.at[:, cols], h_s.at[0, kc], h_r.at[0, kc])
        sndp[0:128, cols] = (dp[0:128, cols] + r1p[:, cols].astype(F32)).astype(BF16)
        send(sndp.at[0:128, cols], recp.at[0:128, cols], e_s.at[0, kc], e_r.at[0, kc], dev(dx=1))
        arrived(r1m.at[:, cols], h_s.at[1, kc], h_r.at[1, kc])
        sndm[128:256, cols] = (dm[128:256, cols] + r1m[:, cols].astype(F32)).astype(BF16)
        send(sndm.at[128:256, cols], recm.at[128:256, cols], e_s.at[1, kc], e_r.at[1, kc], dev(dx=3))

    for dz in z_order:
        arrived(lz.at[at_z(dz)], lz_s.at[dz], lz_r.at[dz])
    lx[xi] = sum_slots(lz, range(NZ))
    for dx in (1, 2, 3):
        send(lx.at[xi], lx.at[xi], lx_s.at[dx], lx_r.at[NX - dx], dev(dx=dx))

    for dx in (1, 2, 3):
        arrived(inner.at[dx], in_s.at[dx], in_r.at[dx])
    weights = sum_slots(inner, range(NX)) * scale[...] * scale[...]
    own_rows = pl.ds(pl.multiple_of(xi * CHUNK, CHUNK), CHUNK)

    for dx in (1, 2, 3):
        arrived(lx.at[at_x(dx)], lx_s.at[dx], lx_r.at[dx])
    loss_ref[0, 0] = jnp.sum(sum_slots(lx, range(NX))) * (-1.0 / (2.0 * ROWS))

    for kc in range(CHUNKS):
        cols = slice(kc * CHUNK, (kc + 1) * CHUNK)
        arrived(recp.at[128:256, cols], d_s.at[0, kc], d_r.at[0, kc])
        arrived(recm.at[0:128, cols], d_s.at[1, kc], d_r.at[1, kc])
        arrived(recp.at[0:128, cols], e_s.at[0, kc], e_r.at[0, kc])
        arrived(recm.at[128:256, cols], e_s.at[1, kc], e_r.at[1, kc])
        delta = down[:, cols] + recp[:, cols].astype(F32) + recm[:, cols].astype(F32)
        grad_ref[:, cols] = scale[:, cols] * (delta - pv[own_rows, cols].astype(F32) * weights[:, cols])

    for cp in sends:
        cp.wait_send()


def me_slot(y, c):
    return y * NC + c


def per_device(features, prototypes):
    vmem = pltpu.VMEM
    dma = pltpu.SemaphoreType.DMA
    grad, loss = pl.pallas_call(
        kernel,
        out_shape=(jax.ShapeDtypeStruct((CHUNK, KD), F32), jax.ShapeDtypeStruct((1, 1), F32)),
        in_specs=[pl.BlockSpec(memory_space=pl.ANY)] * 2,
        out_specs=(pl.BlockSpec(memory_space=pltpu.VMEM), pl.BlockSpec(memory_space=pltpu.SMEM)),
        scratch_shapes=[
            vmem((VIEWS, NY, NZ, NC, PIECE, RD), BF16),
            vmem((D, KD), BF16),
            vmem((KD, D), BF16),
            vmem((VIEWS, KD, RD), F32),
            vmem((VIEWS, KD, RD), F32),
            vmem((VIEWS, KD, RD), BF16),
            vmem((1, KD), F32),
            vmem((VIEWS, 1, RD), F32),
            vmem((VIEWS, 8, 128), F32),
            vmem((2, VIEWS, 8, 128), F32),
            vmem((ITERS, NX, VIEWS, 8, 128), F32),
            vmem((ITERS, NY * NC, 4, 8, 128), F32),
            vmem((ITERS, NZ, 4, 8, 128), F32),
            vmem((NX, 8, 128), F32),
            vmem((NY * NC, 8, 128), F32),
            vmem((NZ, 8, 128), F32),
            vmem((NX, 1, KD), F32),
            vmem((CHUNK, KD), BF16),
            vmem((CHUNK, KD), BF16),
            vmem((CHUNK, KD), BF16),
            vmem((CHUNK // 2, KD), BF16),
            vmem((CHUNK // 2, KD), BF16),
            vmem((CHUNK, KD), BF16),
            vmem((CHUNK, KD), BF16),
            vmem((CHUNK, KD), F32),
            vmem((CHUNK, KD), F32),
            vmem((CHUNK, KD), F32),
            dma((2,)),
            dma((NZ,)), dma((NZ,)),
            dma((2, NZ)), dma((NY, NZ)),
            dma((2, NZ)), dma((2, NZ)),
            dma((NY, NZ)), dma((NY, NZ)),
            dma((ITERS, NX)), dma((ITERS, NX)),
            dma((ITERS, 7)), dma((ITERS, 7)),
            dma((ITERS, NZ)), dma((ITERS, NZ)),
            dma((NX,)), dma((NX,)),
            dma((7,)), dma((7,)),
            dma((NZ,)), dma((NZ,)),
            dma((NX,)), dma((NX,)),
            dma((2, CHUNKS)), dma((2, CHUNKS)),
            dma((2, CHUNKS)), dma((2, CHUNKS)),
            dma((2, CHUNKS)), dma((2, CHUNKS)),
        ],
        compiler_params=pltpu.CompilerParams(
            collective_id=0, has_side_effects=True, vmem_limit_bytes=56 * 2**20
        ),
    )(features.transpose(0, 2, 1), prototypes)
    return grad, loss[0, 0]


def solution(mesh):
    placed = (P(None, "batch", "proto"), P(None, "proto"))
    return jax.shard_map(
        per_device,
        mesh=mesh,
        in_specs=placed,
        out_specs=(P("batch", "proto"), P()),
        check_vma=False,
    )
```

time: 808 us -> 122 us (0.15)
  blocking collectives: 600 us -> 0 us
  Pallas kernels: 0 us -> 117 us
  waiting for transfers between devices: 101 us -> 0 us
  matrix products: 65 us -> 0 us
  other arithmetic: 18.6 us -> 0 us
  between operations: 16 us -> 2.33 us
    psum x7 -> x0, blocking collectives: 600 us -> none  [the longest x3 499 us: per_device(): sample_factor = 1.0 / lax.psum(sample_sum, 'proto')]
    pallas_call x0 -> x1, Pallas kernels: none -> 117 us  [per_device(): pl.pallas_call(kernel, out_shape=(jax.ShapeDtypeStruct((CHUNK, KD), F32),...]
    all_gather x1 -> x0, waiting for transfers between devices: 82.9 us -> none  [per_device(): gathered = lax.all_gather(features, 'proto', axis=2, tiled=True)]
    dot_general x8 -> x0, matrix products: 65 us -> none  [the longest x3 29 us: per_device(): jnp.einsum('vbk,vb->vk', kernel, sample_factor, precision=highest)]
    psum x1 -> x0, waiting for transfers between devices: 17 us -> none  [per_device(): summed = lax.psum(proto_delta, 'batch')]
    reduce_sum x4 -> x0, other arithmetic: 12.6 us -> none  [the longest x1 5.9 us: per_device(): local_loss = jnp.sum(traded_prediction_cost * logarithmic_probabilities)]
  transfers between devices with their start and end apart: 2 -> 0, of which waited for: 2 -> 0; matrix products, arithmetic and copies ran while one was open for 0% -> 0% of each run, Pallas kernels for 0% -> 0%
where the time goes in v1:
time: 122 us
  Pallas kernels  117 us (96%)
  between operations  2.33 us (2%)
  local copies, waits for them, and re-layouts  2.31 us (2%)
    pallas_call x1, Pallas kernels, per_device(): pl.pallas_call(kernel, out_shape=(jax.ShapeDtypeStruct((CHUNK, KD), F32),...  117 us

profile of v1, /device:TPU:1, one launch (start us, length us, event | category | flops | bytes accessed | tf_op | source)
XLA Modules:
  0.0 122.1 jit_solution(6103971181293826393)
XLA Ops:
  0.6 117.5 %shard_map.41 = (f32[256,1024]{1,0:T(8,128)}, f32[1,1]{1,0:T(1,128)}) custom-call(bf16[2,16,1024]{2,1,0:T(8,128)(2,1)} %bitcast.2, bf16[1024,1024]{1,0:T(8,128)(2,1)} %proto_ref.1), custom_call_target="tpu_custom_call" | custom-call | tf_op jit(solution)/shard_map/pallas_call | solution.py:343
  118.1 2.3 %copy.6 = f32[256,1024]{1,0:T(8,128)} copy(f32[256,1024]{1,0:T(8,128)} %get-tuple-element.8) | data formatting | bytes 2097152

commit v2 on v1

--- a/solution.py
+++ b/solution.py
@@ -18,15 +18,24 @@
 PIECE = 16
 CHUNK = 256
 CHUNKS = KD // CHUNK
+LANES = 256
+BLOCKS = RD // LANES
 HEAT = 10.0
 EXP2_SCALE = 10.0 * math.log2(math.e)
 F32 = jnp.float32
 BF16 = jnp.bfloat16
 NT = (((1,), (1,)), ((), ()))
+EARLY, LATE = (0, 1, 7, 2), (6, 3, 5, 4)
+GROUPS = (
+    tuple((0, dz) for dz in EARLY + LATE),
+    tuple((dy, dz) for dy in (1, 3) for dz in EARLY),
+    tuple((dy, dz) for dy in (1, 3) for dz in LATE),
+    tuple((2, dz) for dz in EARLY + LATE),
+)
 
 
 def kernel(feat_ref, proto_ref, grad_ref, loss_ref, ft, pv, ut, sc, kn, sg, scale, rscale, tot, part, xbuf, ybuf, zbuf,
-           lx, ly, lz, inner, snd2, sndp, sndm, r1p, r1m, recp, recm, dp, dm, down,
+           mass, lx, ly, lz, inner, snd2, sndp, sndm, r1p, r1m, recp, recm, dp, dm, down,
            in_sem, z_s, z_r, y_s, y_r, f_s, f_r, c_s, c_r, xs_s, xs_r, ys_s, ys_r, zs_s, zs_r,
            lx_s, lx_r, ly_s, ly_r, lz_s, lz_r, in_s, in_r, h_s, h_r, d_s, d_r, e_s, e_r):
     xi = lax.axis_index("batch")
@@ -47,8 +56,9 @@
     def dev(dx=0, dy=0, dz=0, dc=0):
         return ((at_y(dy) * NZ + at_z(dz)) * NC + lax.rem(c + dc, NC), at_x(dx))
 
-    yc_peers = [(dy, dc) for dy in range(NY) for dc in range(NC) if dy or dc]
+    yc_peers = [(dy, dc) for dy in (2, 1, 3, 0) for dc in range(NC) if dy or dc]
     z_order = [1, 7, 2, 6, 3, 5, 4]
+    z_far = z_order[::-1]
 
     load_p = pltpu.make_async_copy(proto_ref, pv, in_sem.at[0])
     load_p.start()
@@ -70,14 +80,18 @@
     sq = lax.fori_loop(0, D // 16, square_step, jnp.zeros((16, KD), F32))
     scale[...] = lax.rsqrt(jnp.sum(sq, axis=0, keepdims=True) + 1e-6)
 
-    def unit_step(i, _):
-        rows = pl.ds(pl.multiple_of(i * 128, 128), 128)
-        for kb in range(KD // 128):
-            cols = slice(kb * 128, kb * 128 + 128)
-            ut[cols, rows] = (pv[rows, cols].astype(F32) * scale[:, cols]).T.astype(BF16)
+    def piece_rows(dy, dz):
+        return pl.ds(pl.multiple_of((at_y(dy) * NZ + at_z(dz)) * 32, 32), 32)
+
+    def unit_step(kb, _):
+        cols = pl.ds(pl.multiple_of(kb * 128, 128), 128)
+        for i in range(D // 128):
+            four = [p for group in GROUPS for p in group][i * 4:i * 4 + 4]
+            block = jnp.concatenate([pv[piece_rows(dy, dz), cols] for dy, dz in four], axis=0)
+            ut[cols, i * 128:(i + 1) * 128] = (block.astype(F32) * scale[:, cols]).T.astype(BF16)
         return 0
 
-    lax.fori_loop(0, D // 128, unit_step, 0)
+    lax.fori_loop(0, KD // 128, unit_step, 0)
     load_f.wait()
     pl.semaphore_wait(barrier, len(peers))
 
@@ -102,17 +116,16 @@
     def to_sibling(dy, dz):
         send(piece(dy, dz), piece(dy, dz), c_s.at[dy, dz], c_r.at[dy, dz], dev(dc=1))
 
+    def from_sibling(g):
+        for dy, dz in GROUPS[g]:
+            arrived(piece(dy, dz, 1 - c), c_s.at[0, 0], c_r.at[dy, dz])
+
     def along_y(dz):
         for side, dy in ((0, 1), (1, 3)):
             send(piece(0, dz), piece(0, dz), y_s.at[side, dz], y_r.at[(-dy) % NY, dz], dev(dy=dy))
 
     def half(dy, dz, view):
         return ft.at[view, at_y(dy), at_z(dz), c]
-
-    along_y(0)
-    for dz in z_order:
-        send(piece(0, 0), piece(0, 0), z_s.at[dz], z_r.at[(-dz) % NZ], dev(dz=dz))
-    to_sibling(0, 0)
 
     def pass_on_y(dz):
         for side, dy in ((0, 3), (1, 1)):
@@ -120,54 +133,95 @@
             send(half(dy, dz, side), half(dy, dz, side), f_s.at[side, dz], f_r.at[side, dz], dev(dy=-dy))
             to_sibling(dy, dz)
 
-    pass_on_y(0)
-    for i, dz in enumerate(z_order):
+    def from_z(dz):
         arrived(piece(0, dz), z_s.at[0], z_r.at[dz])
         along_y(dz)
         to_sibling(0, dz)
-    for dz in z_order:
-        pass_on_y(dz)
-    for dz in [0] + z_order:
+
+    def opposite(dz):
         for side in range(2):
             arrived(half(2, dz, side), f_s.at[0, 0], f_r.at[side, dz])
         to_sibling(2, dz)
-    for dy in (0, 1, 3, 2):
-        for dz in [0] + z_order:
-            arrived(piece(dy, dz, 1 - c), c_s.at[0, 0], c_r.at[dy, dz])
-
-    def row_square(i, acc):
-        new = []
-        for v in range(VIEWS):
-            val = ft[v, lax.div(i, 16), lax.rem(lax.div(i, 2), 8), lax.rem(i, 2)].astype(F32)
-            new.append(acc[v] + val * val)
-        return tuple(new)
-
-    acc = lax.fori_loop(0, D // PIECE, row_square, (jnp.zeros((16, RD), F32),) * 2)
+
+    def group_dot(g, v, bb):
+        lanes = pl.ds(pl.multiple_of(bb * LANES, LANES), LANES)
+        rhs = jnp.concatenate(
+            [ft[v, at_y(dy), at_z(dz), :, :, lanes].reshape(NC * PIECE, LANES) for dy, dz in GROUPS[g]], axis=0
+        )
+        return lanes, jnp.dot(ut[:, g * CHUNK:(g + 1) * CHUNK], rhs, preferred_element_type=F32)
+
+    def group_scores(g, v):
+        def step(bb, _):
+            lanes, d = group_dot(g, v, bb)
+            if g == 0:
+                sc[v, :, lanes] = d
+            else:
+                sc[v, :, lanes] += d
+            return 0
+
+        lax.fori_loop(0, BLOCKS, step, 0)
+
+    def group_squares(g):
+        def step(bb, _):
+            lanes = pl.ds(pl.multiple_of(bb * 128, 128), 128)
+            for v in range(VIEWS):
+                total = jnp.zeros((PIECE, 128), F32)
+                for dy, dz in GROUPS[g]:
+                    for core in range(NC):
+                        val = ft[v, at_y(dy), at_z(dz), core, :, lanes].astype(F32)
+                        total = total + val * val
+                total = jnp.sum(total, axis=0, keepdims=True)
+                rscale[v, :, lanes] = total if g == 0 else rscale[v, :, lanes] + total
+            return 0
+
+        lax.fori_loop(0, RD // 128, step, 0)
+
+    along_y(0)
+    for dz in z_order:
+        send(piece(0, 0), piece(0, 0), z_s.at[dz], z_r.at[(-dz) % NZ], dev(dz=dz))
+    to_sibling(0, 0)
+    from_z(1)
+    from_z(7)
+    pass_on_y(0)
+    opposite(0)
+    from_z(2)
+    from_z(6)
+    pass_on_y(1)
+    pass_on_y(7)
+    from_z(3)
+    from_z(5)
+    from_z(4)
+    pass_on_y(2)
+    opposite(1)
+    from_sibling(0)
+    group_scores(0, 0)
+    pass_on_y(6)
+    opposite(7)
+    from_sibling(1)
+    group_scores(0, 1)
+    pass_on_y(3)
+    group_scores(1, 0)
+    pass_on_y(5)
+    group_scores(1, 1)
+    pass_on_y(4)
+    group_squares(0)
+    group_squares(1)
+    opposite(2)
+    opposite(6)
+    from_sibling(2)
+    group_scores(2, 0)
+    opposite(3)
+    opposite(5)
+    group_scores(2, 1)
+    opposite(4)
+    group_squares(2)
+    from_sibling(3)
+    group_squares(3)
     for v in range(VIEWS):
-        rscale[v] = lax.rsqrt(jnp.sum(acc[v], axis=0, keepdims=True) + 1e-6)
+        rscale[v] = lax.rsqrt(rscale[v] + 1e-6)
 
     def lane_sum_row(tiles):
         return jnp.sum(tiles.T, axis=0, keepdims=True)
-
-    tot[...] = jnp.zeros_like(tot)
-    for v in range(VIEWS):
-        def score_step(i, _, v=v):
-            rows = pl.ds(pl.multiple_of(i * 128, 128), 128)
-            raw = jnp.dot(ut[rows, :], ft[v].reshape(D, RD), preferred_element_type=F32)
-            s = raw * rscale[v]
-            sc[v, rows, :] = s
-            e = jnp.exp2(s * EXP2_SCALE)
-            k = e * e
-            kn[v, rows, :] = k
-            mass = k[:, 0:128]
-            for j in range(1, RD // 128):
-                mass = mass + k[:, j * 128:(j + 1) * 128]
-            xbuf[0, 0, v, pl.ds(i, 1), :] = lane_sum_row(mass)
-            for j in range(RD // 128):
-                tot[v, j:j + 1, :] += jnp.sum(e[:, j * 128:(j + 1) * 128], axis=0, keepdims=True)
-            return 0
-
-        lax.fori_loop(0, KD // 128, score_step, 0)
 
     def column(buf, v, kb):
         return jnp.broadcast_to(buf[v, pl.ds(kb, 1), :], (128, 128)).T
@@ -178,57 +232,104 @@
             total = total + buf[i]
         return total
 
-    for t in range(ITERS):
-        if t:
-            for v in range(VIEWS):
-                def mass_step(i, _, v=v):
-                    rows = pl.ds(pl.multiple_of(i * 128, 128), 128)
-                    mass = kn[v, rows, 0:128] * part[0, v, 0:1, :]
-                    for j in range(1, RD // 128):
-                        mass = mass + kn[v, rows, j * 128:(j + 1) * 128] * part[0, v, j:j + 1, :]
-                    xbuf[t, 0, v, pl.ds(i, 1), :] = lane_sum_row(mass)
-                    return 0
-
-                lax.fori_loop(0, KD // 128, mass_step, 0)
-        for dx in (1, 2, 3):
-            send(xbuf.at[t, 0], xbuf.at[t, NX - dx], xs_s.at[t, dx], xs_r.at[t, NX - dx], dev(dx=dx))
-        for dx in (1, 2, 3):
-            arrived(xbuf.at[t, dx], xs_s.at[t, dx], xs_r.at[t, dx])
-        part[1] = 1.0 / sum_slots(xbuf.at[t], range(NX))
-        for v in range(VIEWS):
-            def sample_step(i, acc, v=v):
-                rows = pl.ds(pl.multiple_of(i * 128, 128), 128)
-                col = column(part.at[1], v, i)
-                return tuple(
+    def last_scores(v):
+        def step(bb, _):
+            lanes, d = group_dot(3, v, bb)
+            s = (sc[v, :, lanes] + d) * rscale[v, :, lanes]
+            sc[v, :, lanes] = s
+            e = jnp.exp2(s * EXP2_SCALE)
+            k = e * e
+            kn[v, :, lanes] = k
+            mass[...] += k[:, 0:128] + k[:, 128:256]
+            for j in range(LANES // 128):
+                tot[v, pl.ds(bb * 2 + j, 1), :] = jnp.sum(e[:, j * 128:(j + 1) * 128], axis=0, keepdims=True)
+            return 0
+
+        mass[...] = jnp.zeros_like(mass)
+        lax.fori_loop(0, BLOCKS, step, 0)
+        for i in range(KD // 128):
+            xbuf[0, v, 0, i:i + 1, :] = lane_sum_row(mass[i * 128:(i + 1) * 128, :])
+
+    def proto_mass(t, v):
+        def step(i, _):
+            for kb in (i * 2, i * 2 + 1):
+                rows = pl.ds(pl.multiple_of(kb * 128, 128), 128)
+                total = kn[v, rows, 0:128] * part[0, v, 0:1, :]
+                for j in range(1, RD // 128):
+                    total = total + kn[v, rows, j * 128:(j + 1) * 128] * part[0, v, j:j + 1, :]
+                xbuf[t, v, 0, pl.ds(kb, 1), :] = lane_sum_row(total)
+            return 0
+
+        lax.fori_loop(0, KD // 256, step, 0)
+
+    def send_x(t, v):
+        for dx in (2, 1, 3):
+            send(xbuf.at[t, v, 0], xbuf.at[t, v, NX - dx], xs_s.at[t, v, dx], xs_r.at[t, v, NX - dx], dev(dx=dx))
+
+    def sample_mass(t, v):
+        for dx in (1, 3, 2):
+            arrived(xbuf.at[t, v, dx], xs_s.at[t, v, dx], xs_r.at[t, v, dx])
+        part[1, v] = 1.0 / sum_slots(xbuf.at[t, v], range(NX))
+
+        def step(i, acc):
+            for kb in (i * 2, i * 2 + 1):
+                rows = pl.ds(pl.multiple_of(kb * 128, 128), 128)
+                col = column(part.at[1], v, kb)
+                acc = tuple(
                     acc[j] + jnp.sum((kn[v, rows, j * 128:(j + 1) * 128] * col).reshape(16, 8, 128), axis=0)
                     for j in range(RD // 128)
                 )
-
-            acc = lax.fori_loop(0, KD // 128, sample_step, (jnp.zeros((8, 128), F32),) * 8)
-            for j in range(RD // 128):
-                ybuf[t, 0, v, j:j + 1, :] = jnp.sum(acc[j], axis=0, keepdims=True)
+            return acc
+
+        acc = lax.fori_loop(0, KD // 256, step, (jnp.zeros((8, 128), F32),) * 8)
+        for j in range(RD // 128):
+            ybuf[t, v, 0, 0, j:j + 1, :] = jnp.sum(acc[j], axis=0, keepdims=True)
         if t == 0:
-            ybuf[t, 0, 2:4] = tot[...]
-        n = 4 if t == 0 else 2
+            ybuf[t, v, 0, 1] = tot[v]
+
+    def send_y(t, v):
+        n = 2 if t == 0 else 1
         for i, (dy, dc) in enumerate(yc_peers):
             j = yc_peers.index(((-dy) % NY, dc))
-            send(ybuf.at[t, 0, 0:n], ybuf.at[t, 1 + j, 0:n], ys_s.at[t, i], ys_r.at[t, j], dev(dy=dy, dc=dc))
+            send(ybuf.at[t, v, 0, 0:n], ybuf.at[t, v, 1 + j, 0:n], ys_s.at[t, v, i], ys_r.at[t, v, j], dev(dy=dy, dc=dc))
+
+    def send_z(t, v):
+        n = 2 if t == 0 else 1
         for i in range(len(yc_peers)):
-            arrived(ybuf.at[t, 1 + i, 0:n], ys_s.at[t, i], ys_r.at[t, i])
-        zbuf[t, 0, 0:n] = sum_slots(ybuf.at[t, :, 0:n], range(8))
+            arrived(ybuf.at[t, v, 1 + i, 0:n], ys_s.at[t, v, i], ys_r.at[t, v, i])
+        zbuf[t, v, 0, 0:n] = sum_slots(ybuf.at[t, v, :, 0:n], range(8))
+        for dz in z_far:
+            send(zbuf.at[t, v, 0, 0:n], zbuf.at[t, v, NZ - dz, 0:n], zs_s.at[t, v, dz], zs_r.at[t, v, NZ - dz], dev(dz=dz))
+
+    def take_z(t, v):
+        n = 2 if t == 0 else 1
         for dz in z_order:
-            send(zbuf.at[t, 0, 0:n], zbuf.at[t, NZ - dz, 0:n], zs_s.at[t, dz], zs_r.at[t, NZ - dz], dev(dz=dz))
-        for dz in z_order:
-            arrived(zbuf.at[t, dz, 0:n], zs_s.at[t, dz], zs_r.at[t, dz])
-        sums = sum_slots(zbuf.at[t, :, 0:n], range(NZ))
-        part[0] = 1.0 / sums[0:2]
+            arrived(zbuf.at[t, v, dz, 0:n], zs_s.at[t, v, dz], zs_r.at[t, v, dz])
+        sums = sum_slots(zbuf.at[t, v, :, 0:n], range(NZ))
+        part[0, v] = 1.0 / sums[0]
         if t == 0:
-            tot[...] = sums[2:4]
+            tot[v] = sums[1]
+
+    for t in range(ITERS):
+        for v in range(VIEWS):
+            if t == 0:
+                last_scores(v)
+            else:
+                take_z(t - 1, v)
+                proto_mass(t, v)
+            send_x(t, v)
+        for v in range(VIEWS):
+            sample_mass(t, v)
+            send_y(t, v)
+        for v in range(VIEWS):
+            send_z(t, v)
+    for v in range(VIEWS):
+        take_z(ITERS - 1, v)
 
     factor, proto_factor = part.at[0], part.at[1]
     loss_acc = jnp.zeros((8, 128), F32)
     for v in range(VIEWS):
-        loss_acc += jnp.log(tot[v]) * factor[1 - v] * ybuf[ITERS - 1, 0, 1 - v]
+        loss_acc += jnp.log(tot[v]) * factor[1 - v] * ybuf[ITERS - 1, 1 - v, 0, 0]
     loss_acc = -loss_acc
 
     def grad_block(dx, cols):
@@ -356,9 +457,10 @@
             vmem((VIEWS, 1, RD), F32),
             vmem((VIEWS, 8, 128), F32),
             vmem((2, VIEWS, 8, 128), F32),
-            vmem((ITERS, NX, VIEWS, 8, 128), F32),
-            vmem((ITERS, NY * NC, 4, 8, 128), F32),
-            vmem((ITERS, NZ, 4, 8, 128), F32),
+            vmem((ITERS, VIEWS, NX, 8, 128), F32),
+            vmem((ITERS, VIEWS, NY * NC, 2, 8, 128), F32),
+            vmem((ITERS, VIEWS, NZ, 2, 8, 128), F32),
+            vmem((KD, 128), F32),
             vmem((NX, 8, 128), F32),
             vmem((NY * NC, 8, 128), F32),
             vmem((NZ, 8, 128), F32),
@@ -378,9 +480,9 @@
             dma((2, NZ)), dma((NY, NZ)),
             dma((2, NZ)), dma((2, NZ)),
             dma((NY, NZ)), dma((NY, NZ)),
-            dma((ITERS, NX)), dma((ITERS, NX)),
-            dma((ITERS, 7)), dma((ITERS, 7)),
-            dma((ITERS, NZ)), dma((ITERS, NZ)),
+            dma((ITERS, VIEWS, NX)), dma((ITERS, VIEWS, NX)),
+            dma((ITERS, VIEWS, 7)), dma((ITERS, VIEWS, 7)),
+            dma((ITERS, VIEWS, NZ)), dma((ITERS, VIEWS, NZ)),
             dma((NX,)), dma((NX,)),
             dma((7,)), dma((7,)),
             dma((NZ,)), dma((NZ,)),

time: 122 us -> 110 us (0.902)
  Pallas kernels: 117 us -> 105 us
    pallas_call x1, Pallas kernels: 117 us -> 105 us  [per_device(): pl.pallas_call(kernel, out_shape=(jax.ShapeDtypeStruct((CHUNK, KD), F32),...]
where the time goes in v2:
time: 110 us
  Pallas kernels  105 us (95%)
  between operations  2.33 us (2%)
  local copies, waits for them, and re-layouts  2.31 us (2%)
    pallas_call x1, Pallas kernels, per_device(): pl.pallas_call(kernel, out_shape=(jax.ShapeDtypeStruct((CHUNK, KD), F32),...  105 us
    unnamed x1, local copies, waits for them, and re-layouts  2.31 us

profile of v2, /device:TPU:1, one launch (start us, length us, event | category | flops | bytes accessed | tf_op | source)
XLA Modules:
  0.0 109.6 jit_solution(8866507899113239505)
XLA Ops:
  0.6 105.0 %shard_map.41 = (f32[256,1024]{1,0:T(8,128)}, f32[1,1]{1,0:T(1,128)}) custom-call(bf16[2,16,1024]{2,1,0:T(8,128)(2,1)} %bitcast.2, bf16[1024,1024]{1,0:T(8,128)(2,1)} %proto_ref.1), custom_call_target="tpu_custom_call" | custom-call | tf_op jit(solution)/shard_map/pallas_call | solution.py:444
  105.6 2.3 %copy.6 = f32[256,1024]{1,0:T(8,128)} copy(f32[256,1024]{1,0:T(8,128)} %get-tuple-element.8) | data formatting | bytes 2097152

commit v3 on v2

--- a/solution.py
+++ b/solution.py
@@ -25,13 +25,10 @@
 F32 = jnp.float32
 BF16 = jnp.bfloat16
 NT = (((1,), (1,)), ((), ()))
-EARLY, LATE = (0, 1, 7, 2), (6, 3, 5, 4)
-GROUPS = (
-    tuple((0, dz) for dz in EARLY + LATE),
-    tuple((dy, dz) for dy in (1, 3) for dz in EARLY),
-    tuple((dy, dz) for dy in (1, 3) for dz in LATE),
-    tuple((2, dz) for dz in EARLY + LATE),
-)
+Y_PLACES = (0, 1, 3, 2)
+Z_PLACES = (0, 1, 7, 2, 6, 3, 5, 4)
+STEPS = ((0, 1), (1, 3), (3, 5), (5, 7), (7, 8))
+GROUPS = (((0, 1), (0, 8)), ((1, 3), (0, 4)), ((1, 3), (4, 8)), ((3, 4), (0, 8)))
 
 
 def kernel(feat_ref, proto_ref, grad_ref, loss_ref, ft, pv, ut, sc, kn, sg, scale, rscale, tot, part, xbuf, ybuf, zbuf,
@@ -62,7 +59,7 @@
 
     load_p = pltpu.make_async_copy(proto_ref, pv, in_sem.at[0])
     load_p.start()
-    load_f = pltpu.make_async_copy(feat_ref, ft.at[:, y, z, c], in_sem.at[1])
+    load_f = pltpu.make_async_copy(feat_ref, ft.at[:, 0, 0, c], in_sem.at[1])
     load_f.start()
 
     barrier = pltpu.get_barrier_semaphore()
@@ -80,14 +77,18 @@
     sq = lax.fori_loop(0, D // 16, square_step, jnp.zeros((16, KD), F32))
     scale[...] = lax.rsqrt(jnp.sum(sq, axis=0, keepdims=True) + 1e-6)
 
-    def piece_rows(dy, dz):
-        return pl.ds(pl.multiple_of((at_y(dy) * NZ + at_z(dz)) * 32, 32), 32)
+    order = [
+        (Y_PLACES[i], Z_PLACES[j]) for ys, zs in GROUPS for i in range(*ys) for j in range(*zs)
+    ]
+
+    def feature_rows(row_block, dz):
+        return pl.ds(pl.multiple_of((row_block * NZ + at_z(dz)) * 32, 32), 32)
 
     def unit_step(kb, _):
         cols = pl.ds(pl.multiple_of(kb * 128, 128), 128)
         for i in range(D // 128):
-            four = [p for group in GROUPS for p in group][i * 4:i * 4 + 4]
-            block = jnp.concatenate([pv[piece_rows(dy, dz), cols] for dy, dz in four], axis=0)
+            four = order[i * 4:i * 4 + 4]
+            block = jnp.concatenate([pv[feature_rows(at_y(dy), dz), cols] for dy, dz in four], axis=0)
             ut[cols, i * 128:(i + 1) * 128] = (block.astype(F32) * scale[:, cols]).T.astype(BF16)
         return 0
 
@@ -110,44 +111,45 @@
     def arrived(dst, ssem, rsem):
         copy(dst, dst, ssem, rsem, dev(dc=1)).wait_recv()
 
-    def piece(dy, dz, core=None):
-        return ft.at[:, at_y(dy), at_z(dz), c if core is None else core]
-
-    def to_sibling(dy, dz):
-        send(piece(dy, dz), piece(dy, dz), c_s.at[dy, dz], c_r.at[dy, dz], dev(dc=1))
-
-    def from_sibling(g):
-        for dy, dz in GROUPS[g]:
-            arrived(piece(dy, dz, 1 - c), c_s.at[0, 0], c_r.at[dy, dz])
-
-    def along_y(dz):
-        for side, dy in ((0, 1), (1, 3)):
-            send(piece(0, dz), piece(0, dz), y_s.at[side, dz], y_r.at[(-dy) % NY, dz], dev(dy=dy))
-
-    def half(dy, dz, view):
-        return ft.at[view, at_y(dy), at_z(dz), c]
-
-    def pass_on_y(dz):
-        for side, dy in ((0, 3), (1, 1)):
-            arrived(piece(dy, dz), y_s.at[0, 0], y_r.at[dy, dz])
-            send(half(dy, dz, side), half(dy, dz, side), f_s.at[side, dz], f_r.at[side, dz], dev(dy=-dy))
-            to_sibling(dy, dz)
-
-    def from_z(dz):
-        arrived(piece(0, dz), z_s.at[0], z_r.at[dz])
-        along_y(dz)
-        to_sibling(0, dz)
-
-    def opposite(dz):
+    def part_of(ys, zs, core=None):
+        return ft.at[:, ys[0]:ys[1], zs[0]:zs[1], c if core is None else core]
+
+    def to_sibling(kind, ys, q):
+        send(part_of(ys, STEPS[q]), part_of(ys, STEPS[q]), c_s.at[kind, q], c_r.at[kind, q], dev(dc=1))
+
+    def from_sibling(kind, steps):
+        ys = ((0, 1), (1, 3), (3, 4))[kind]
+        for q in steps:
+            arrived(part_of(ys, STEPS[q], 1 - c), c_s.at[0, 0], c_r.at[kind, q])
+
+    def along_y(q):
+        for side, dy, place in ((0, 1, 2), (1, 3, 1)):
+            send(part_of((0, 1), STEPS[q]), part_of((place, place + 1), STEPS[q]), y_s.at[side, q], y_r.at[side, q], dev(dy=dy))
+        to_sibling(0, (0, 1), q)
+
+    def half(place, q, view):
+        return ft.at[view, place, STEPS[q][0]:STEPS[q][1], c]
+
+    def pass_on_y(q):
+        for side, dy, place in ((0, 1, 2), (1, 3, 1)):
+            arrived(part_of((place, place + 1), STEPS[q]), y_s.at[0, 0], y_r.at[side, q])
+            send(half(place, q, side), half(3, q, side), f_s.at[side, q], f_r.at[side, q], dev(dy=dy))
+        to_sibling(1, (1, 3), q)
+
+    def from_z(q):
+        for j in range(*STEPS[q]):
+            arrived(part_of((0, 1), (j, j + 1)), z_s.at[0], z_r.at[Z_PLACES[j]])
+        along_y(q)
+
+    def opposite(q):
         for side in range(2):
-            arrived(half(2, dz, side), f_s.at[0, 0], f_r.at[side, dz])
-        to_sibling(2, dz)
+            arrived(half(3, q, side), f_s.at[0, 0], f_r.at[side, q])
+        to_sibling(2, (3, 4), q)
 
     def group_dot(g, v, bb):
         lanes = pl.ds(pl.multiple_of(bb * LANES, LANES), LANES)
-        rhs = jnp.concatenate(
-            [ft[v, at_y(dy), at_z(dz), :, :, lanes].reshape(NC * PIECE, LANES) for dy, dz in GROUPS[g]], axis=0
-        )
+        ys, zs = GROUPS[g]
+        rhs = ft[v, ys[0]:ys[1], zs[0]:zs[1], :, :, lanes].reshape(CHUNK, LANES)
         return lanes, jnp.dot(ut[:, g * CHUNK:(g + 1) * CHUNK], rhs, preferred_element_type=F32)
 
     def group_scores(g, v):
@@ -165,12 +167,9 @@
         def step(bb, _):
             lanes = pl.ds(pl.multiple_of(bb * 128, 128), 128)
             for v in range(VIEWS):
-                total = jnp.zeros((PIECE, 128), F32)
-                for dy, dz in GROUPS[g]:
-                    for core in range(NC):
-                        val = ft[v, at_y(dy), at_z(dz), core, :, lanes].astype(F32)
-                        total = total + val * val
-                total = jnp.sum(total, axis=0, keepdims=True)
+                ys, zs = GROUPS[g]
+                val = ft[v, ys[0]:ys[1], zs[0]:zs[1], :, :, lanes].astype(F32)
+                total = jnp.sum((val * val).reshape(CHUNK, 128), axis=0, keepdims=True)
                 rscale[v, :, lanes] = total if g == 0 else rscale[v, :, lanes] + total
             return 0
 
@@ -178,44 +177,35 @@
 
     along_y(0)
     for dz in z_order:
-        send(piece(0, 0), piece(0, 0), z_s.at[dz], z_r.at[(-dz) % NZ], dev(dz=dz))
-    to_sibling(0, 0)
+        place = Z_PLACES.index(NZ - dz)
+        send(part_of((0, 1), (0, 1)), part_of((0, 1), (place, place + 1)), z_s.at[dz], z_r.at[NZ - dz], dev(dz=dz))
     from_z(1)
-    from_z(7)
     pass_on_y(0)
     opposite(0)
     from_z(2)
-    from_z(6)
     pass_on_y(1)
-    pass_on_y(7)
     from_z(3)
-    from_z(5)
     from_z(4)
+    opposite(1)
     pass_on_y(2)
-    opposite(1)
-    from_sibling(0)
+    from_sibling(0, range(5))
     group_scores(0, 0)
-    pass_on_y(6)
-    opposite(7)
-    from_sibling(1)
     group_scores(0, 1)
     pass_on_y(3)
+    from_sibling(1, range(3))
     group_scores(1, 0)
-    pass_on_y(5)
+    pass_on_y(4)
     group_scores(1, 1)
-    pass_on_y(4)
+    opposite(2)
     group_squares(0)
     group_squares(1)
-    opposite(2)
-    opposite(6)
-    from_sibling(2)
+    from_sibling(1, range(3, 5))
+    opposite(3)
     group_scores(2, 0)
-    opposite(3)
-    opposite(5)
+    opposite(4)
     group_scores(2, 1)
-    opposite(4)
     group_squares(2)
-    from_sibling(3)
+    from_sibling(2, range(5))
     group_squares(3)
     for v in range(VIEWS):
         rscale[v] = lax.rsqrt(rscale[v] + 1e-6)
@@ -260,7 +250,8 @@
                 xbuf[t, v, 0, pl.ds(kb, 1), :] = lane_sum_row(total)
             return 0
 
-        lax.fori_loop(0, KD // 256, step, 0)
+        for i in range(KD // 256):
+            step(i, 0)
 
     def send_x(t, v):
         for dx in (2, 1, 3):
@@ -281,7 +272,9 @@
                 )
             return acc
 
-        acc = lax.fori_loop(0, KD // 256, step, (jnp.zeros((8, 128), F32),) * 8)
+        acc = (jnp.zeros((8, 128), F32),) * 8
+        for i in range(KD // 256):
+            acc = step(i, acc)
         for j in range(RD // 128):
             ybuf[t, v, 0, 0, j:j + 1, :] = jnp.sum(acc[j], axis=0, keepdims=True)
         if t == 0:
@@ -332,17 +325,21 @@
         loss_acc += jnp.log(tot[v]) * factor[1 - v] * ybuf[ITERS - 1, 1 - v, 0, 0]
     loss_acc = -loss_acc
 
+    def y_place(row_block):
+        dy = lax.rem(row_block + NY - y, NY)
+        return dy + lax.div(dy, 2) * (5 - 2 * dy)
+
     def grad_block(dx, cols):
         out = None
         for v in range(VIEWS):
-            lhs = ft[v, at_x(dx)].reshape(CHUNK, RD)
+            lhs = ft[v, y_place(at_x(dx))].reshape(CHUNK, RD)
             d = lax.dot_general(lhs, sg[v, cols, :], NT, preferred_element_type=F32)
             out = d if out is None else out + d
         return out
 
     def weigh(dx, cols, delta):
-        rows = pl.ds(pl.multiple_of(at_x(dx) * CHUNK, CHUNK), CHUNK)
-        return jnp.sum(pv[rows, cols].astype(F32) * delta, axis=0, keepdims=True)
+        own = jnp.concatenate([pv[feature_rows(at_x(dx), dz), cols] for dz in Z_PLACES], axis=0)
+        return jnp.sum(own.astype(F32) * delta, axis=0, keepdims=True)
 
     for kc in range(CHUNKS):
         cols = slice(kc * CHUNK, (kc + 1) * CHUNK)
@@ -415,7 +412,6 @@
     for dx in (1, 2, 3):
         arrived(inner.at[dx], in_s.at[dx], in_r.at[dx])
     weights = sum_slots(inner, range(NX)) * scale[...] * scale[...]
-    own_rows = pl.ds(pl.multiple_of(xi * CHUNK, CHUNK), CHUNK)
 
     for dx in (1, 2, 3):
         arrived(lx.at[at_x(dx)], lx_s.at[dx], lx_r.at[dx])
@@ -428,7 +424,9 @@
         arrived(recp.at[0:128, cols], e_s.at[0, kc], e_r.at[0, kc])
         arrived(recm.at[128:256, cols], e_s.at[1, kc], e_r.at[1, kc])
         delta = down[:, cols] + recp[:, cols].astype(F32) + recm[:, cols].astype(F32)
-        grad_ref[:, cols] = scale[:, cols] * (delta - pv[own_rows, cols].astype(F32) * weights[:, cols])
+        for j, dz in enumerate(Z_PLACES):
+            unit = pv[feature_rows(xi, dz), cols].astype(F32) * weights[:, cols]
+            grad_ref[feature_rows(0, dz), cols] = scale[:, cols] * (delta[j * 32:(j + 1) * 32] - unit)
 
     for cp in sends:
         cp.wait_send()
@@ -443,7 +441,7 @@
     dma = pltpu.SemaphoreType.DMA
     grad, loss = pl.pallas_call(
         kernel,
-        out_shape=(jax.ShapeDtypeStruct((CHUNK, KD), F32), jax.ShapeDtypeStruct((1, 1), F32)),
+        out_shape=(pltpu.VMEM((CHUNK, KD), F32), jax.ShapeDtypeStruct((1, 1), F32)),
         in_specs=[pl.BlockSpec(memory_space=pl.ANY)] * 2,
         out_specs=(pl.BlockSpec(memory_space=pltpu.VMEM), pl.BlockSpec(memory_space=pltpu.SMEM)),
         scratch_shapes=[
@@ -477,9 +475,9 @@
             vmem((CHUNK, KD), F32),
             dma((2,)),
             dma((NZ,)), dma((NZ,)),
-            dma((2, NZ)), dma((NY, NZ)),
-            dma((2, NZ)), dma((2, NZ)),
-            dma((NY, NZ)), dma((NY, NZ)),
+            dma((2, 5)), dma((2, 5)),
+            dma((2, 5)), dma((2, 5)),
+            dma((3, 5)), dma((3, 5)),
             dma((ITERS, VIEWS, NX)), dma((ITERS, VIEWS, NX)),
             dma((ITERS, VIEWS, 7)), dma((ITERS, VIEWS, 7)),
             dma((ITERS, VIEWS, NZ)), dma((ITERS, VIEWS, NZ)),

time: 110 us -> 107 us (0.973)
  Pallas kernels: 105 us -> 103 us
  local copies, waits for them, and re-layouts: 2.31 us -> 0.97 us
    pallas_call x1, Pallas kernels: 105 us -> 103 us  [per_device(): pl.pallas_call(kernel, out_shape=(pltpu.VMEM((CHUNK, KD), F32), jax.Shape...]
    unnamed x1, local copies, waits for them, and re-layouts: 2.31 us -> 0.97 us
where the time goes in v3:
time: 107 us
  Pallas kernels  103 us (96%)
  between operations  2.33 us (2%)
    pallas_call x1, Pallas kernels, per_device(): pl.pallas_call(kernel, out_shape=(pltpu.VMEM((CHUNK, KD), F32), jax.Shape...  103 us

profile of v3, /device:TPU:1, one launch (start us, length us, event | category | flops | bytes accessed | tf_op | source)
XLA Modules:
  0.0 106.7 jit_solution(16432924923943611659)
XLA Ops:
  0.6 103.4 %shard_map.41 = (f32[256,1024]{1,0:T(8,128)S(1)}, f32[1,1]{1,0:T(1,128)}) custom-call(bf16[2,16,1024]{2,1,0:T(8,128)(2,1)} %bitcast.2, bf16[1024,1024]{1,0:T(8,128)(2,1)} %proto_ref.1), custom_call_target="tpu_custom_call" | custom-call | tf_op jit(solution)/shard_map/pallas_call | solution.py:442
  104.0 1.0 copy.6

commit v4 on v3

--- a/solution.py
+++ b/solution.py
@@ -107,6 +107,11 @@
         cp = copy(src, dst, ssem, rsem, to)
         cp.start()
         sends.append(cp)
+
+    def flush(count):
+        for cp in sends[:count]:
+            cp.wait_send()
+        del sends[:count]
 
     def arrived(dst, ssem, rsem):
         copy(dst, dst, ssem, rsem, dev(dc=1)).wait_recv()
@@ -236,7 +241,8 @@
             return 0
 
         mass[...] = jnp.zeros_like(mass)
-        lax.fori_loop(0, BLOCKS, step, 0)
+        for bb in range(BLOCKS):
+            step(bb, 0)
         for i in range(KD // 128):
             xbuf[0, v, 0, i:i + 1, :] = lane_sum_row(mass[i * 128:(i + 1) * 128, :])
 
@@ -304,6 +310,7 @@
             tot[v] = sums[1]
 
     for t in range(ITERS):
+        older = len(sends)
         for v in range(VIEWS):
             if t == 0:
                 last_scores(v)
@@ -311,6 +318,7 @@
                 take_z(t - 1, v)
                 proto_mass(t, v)
             send_x(t, v)
+        flush(older)
         for v in range(VIEWS):
             sample_mass(t, v)
             send_y(t, v)
@@ -318,6 +326,8 @@
             send_z(t, v)
     for v in range(VIEWS):
         take_z(ITERS - 1, v)
+
+    older = len(sends)
 
     factor, proto_factor = part.at[0], part.at[1]
     loss_acc = jnp.zeros((8, 128), F32)
@@ -359,7 +369,7 @@
                     acc = acc + jnp.sum((assign * s).reshape(16, 8, 128), axis=0) * HEAT
             return acc
 
-        loss_acc = lax.fori_loop(0, 2, slope_step, loss_acc)
+        loss_acc = slope_step(1, slope_step(0, loss_acc))
         delta = grad_block(2, cols)
         snd2[:, cols] = delta.astype(BF16)
         inner[0, :, cols] = weigh(2, cols, delta)
@@ -384,6 +394,8 @@
         own = grad_block(0, cols)
         down[:, cols] = own
         inner[0, :, cols] += weigh(1, cols, dplus) + weigh(3, cols, dminus) + weigh(0, cols, own)
+    flush(older)
+    older = len(sends)
     for dx in (1, 2, 3):
         send(inner.at[0], inner.at[NX - dx], in_s.at[dx], in_r.at[NX - dx], dev(dx=dx))
 
@@ -403,6 +415,8 @@
         sndm[128:256, cols] = (dm[128:256, cols] + r1m[:, cols].astype(F32)).astype(BF16)
         send(sndm.at[128:256, cols], recm.at[128:256, cols], e_s.at[1, kc], e_r.at[1, kc], dev(dx=3))
 
+    flush(older)
+    older = len(sends)
     for dz in z_order:
         arrived(lz.at[at_z(dz)], lz_s.at[dz], lz_r.at[dz])
     lx[xi] = sum_slots(lz, range(NZ))
@@ -412,10 +426,6 @@
     for dx in (1, 2, 3):
         arrived(inner.at[dx], in_s.at[dx], in_r.at[dx])
     weights = sum_slots(inner, range(NX)) * scale[...] * scale[...]
-
-    for dx in (1, 2, 3):
-        arrived(lx.at[at_x(dx)], lx_s.at[dx], lx_r.at[dx])
-    loss_ref[0, 0] = jnp.sum(sum_slots(lx, range(NX))) * (-1.0 / (2.0 * ROWS))
 
     for kc in range(CHUNKS):
         cols = slice(kc * CHUNK, (kc + 1) * CHUNK)
@@ -428,8 +438,12 @@
             unit = pv[feature_rows(xi, dz), cols].astype(F32) * weights[:, cols]
             grad_ref[feature_rows(0, dz), cols] = scale[:, cols] * (delta[j * 32:(j + 1) * 32] - unit)
 
-    for cp in sends:
-        cp.wait_send()
+    flush(older)
+    for dx in (1, 2, 3):
+        arrived(lx.at[at_x(dx)], lx_s.at[dx], lx_r.at[dx])
+    loss_ref[0, 0] = jnp.sum(sum_slots(lx, range(NX))) * (-1.0 / (2.0 * ROWS))
+
+    flush(len(sends))
 
 
 def me_slot(y, c):

time: 107 us -> 105 us (0.981)
    pallas_call x1, Pallas kernels: 103 us -> 102 us  [per_device(): pl.pallas_call(kernel, out_shape=(pltpu.VMEM((CHUNK, KD), F32), jax.Shape...]
where the time goes in v4:
time: 105 us
  Pallas kernels  102 us (97%)
  between operations  2.33 us (2%)
    pallas_call x1, Pallas kernels, per_device(): pl.pallas_call(kernel, out_shape=(pltpu.VMEM((CHUNK, KD), F32), jax.Shape...  102 us

profile of v4, /device:TPU:1, one launch (start us, length us, event | category | flops | bytes accessed | tf_op | source)
XLA Modules:
  0.0 105.0 jit_solution(18304835969752749023)
XLA Ops:
  0.6 101.7 %shard_map.41 = (f32[256,1024]{1,0:T(8,128)S(1)}, f32[1,1]{1,0:T(1,128)}) custom-call(bf16[2,16,1024]{2,1,0:T(8,128)(2,1)} %bitcast.2, bf16[1024,1024]{1,0:T(8,128)(2,1)} %proto_ref.1), custom_call_target="tpu_custom_call" | custom-call | tf_op jit(solution)/shard_map/pallas_call | solution.py:456
  102.3 1.0 copy.6

commit v5 on v4

--- a/solution.py
+++ b/solution.py
@@ -31,7 +31,7 @@
 GROUPS = (((0, 1), (0, 8)), ((1, 3), (0, 4)), ((1, 3), (4, 8)), ((3, 4), (0, 8)))
 
 
-def kernel(feat_ref, proto_ref, grad_ref, loss_ref, ft, pv, ut, sc, kn, sg, scale, rscale, tot, part, xbuf, ybuf, zbuf,
+def kernel(feat_ref, proto_ref, grad_ref, loss_ref, ft, pv, ut, sc, kn, pred, sg, scale, rscale, tot, part, xbuf, ybuf, zbuf,
            mass, lx, ly, lz, inner, snd2, sndp, sndm, r1p, r1m, recp, recm, dp, dm, down,
            in_sem, z_s, z_r, y_s, y_r, f_s, f_r, c_s, c_r, xs_s, xs_r, ys_s, ys_r, zs_s, zs_r,
            lx_s, lx_r, ly_s, ly_r, lz_s, lz_r, in_s, in_r, h_s, h_r, d_s, d_r, e_s, e_r):
@@ -309,6 +309,17 @@
         if t == 0:
             tot[v] = sums[1]
 
+    def predict(v):
+        def step(i, _):
+            rows = pl.ds(pl.multiple_of(i * 128, 128), 128)
+            for j in range(RD // 128):
+                lanes = slice(j * 128, (j + 1) * 128)
+                weight = rscale[v, :, lanes] * HEAT / tot[v, j:j + 1, :]
+                pred[v, rows, lanes] = jnp.exp2(sc[v, rows, lanes] * EXP2_SCALE) * weight
+            return 0
+
+        lax.fori_loop(0, KD // 128, step, 0)
+
     for t in range(ITERS):
         older = len(sends)
         for v in range(VIEWS):
@@ -324,6 +335,8 @@
             send_y(t, v)
         for v in range(VIEWS):
             send_z(t, v)
+        if t:
+            predict(t - 1)
     for v in range(VIEWS):
         take_z(ITERS - 1, v)
 
@@ -364,8 +377,7 @@
                     heated = rscale[v, :, lanes] * HEAT
                     s = sc[v, rows, lanes]
                     assign = kn[1 - v, rows, lanes] * col * factor[1 - v, j:j + 1, :]
-                    pred = jnp.exp2(s * EXP2_SCALE) * (heated / tot[v, j:j + 1, :])
-                    sg[v, rows, lanes] = (pred - assign * heated).astype(BF16)
+                    sg[v, rows, lanes] = (pred[v, rows, lanes] - assign * heated).astype(BF16)
                     acc = acc + jnp.sum((assign * s).reshape(16, 8, 128), axis=0) * HEAT
             return acc
 
@@ -462,6 +474,7 @@
             vmem((VIEWS, NY, NZ, NC, PIECE, RD), BF16),
             vmem((D, KD), BF16),
             vmem((KD, D), BF16),
+            vmem((VIEWS, KD, RD), F32),
             vmem((VIEWS, KD, RD), F32),
             vmem((VIEWS, KD, RD), F32),
             vmem((VIEWS, KD, RD), BF16),

time: 105 us -> 104 us (level)
  no operation moved by 1% of the time
where the time goes in v5:
time: 104 us
  Pallas kernels  101 us (97%)
  between operations  2.33 us (2%)
    pallas_call x1, Pallas kernels, per_device(): pl.pallas_call(kernel, out_shape=(pltpu.VMEM((CHUNK, KD), F32), jax.Shape...  101 us

profile of v5, /device:TPU:1, one launch (start us, length us, event | category | flops | bytes accessed | tf_op | source)
XLA Modules:
  0.0 104.2 jit_solution(8592874149138056348)
XLA Ops:
  0.6 100.9 %shard_map.41 = (f32[256,1024]{1,0:T(8,128)S(1)}, f32[1,1]{1,0:T(1,128)}) custom-call(bf16[2,16,1024]{2,1,0:T(8,128)(2,1)} %bitcast.2, bf16[1024,1024]{1,0:T(8,128)(2,1)} %proto_ref.1), custom_call_target="tpu_custom_call" | custom-call | tf_op jit(solution)/shard_map/pallas_call | solution.py:468
  101.5 1.0 copy.6
